TPU v7x, 256 devices: a whole 4x4x8 slice. The times are simulated.
256 devices in a mesh: row: 8 (over x, y_hi), col: 16 (over z, core), rep: 2 (over y_lo).
Axes of the slice: x: 4, y: 4 (y_hi: 2, y_lo: 2; y = y_hi * 2 + y_lo), z: 8, core: 2. Of those that a mesh axis runs over, the one named last changes fastest.
Arguments:
- grad_out: float32 [65536, 256], P(('row', 'col', 'rep')), may hold values from -6 to 6
- tile_vals: bfloat16 [98304, 128, 128], P(('row', 'col', 'rep')), may hold values from 0.0039978027 to 0.039794922
- tile_rows: int32 [98304], P(('row', 'col', 'rep')), may hold values from 0 to 63
- tile_cols: int32 [98304], P(('row', 'col', 'rep')), may hold values from 0 to 31
- tile_counts: int32 [256], P(('row', 'col', 'rep')), may hold values from 1 to 384, as said below
Outputs:
- grad_in: float32 [65536, 256], P(('col', 'row', 'rep'))
Inputs may be any that keep to these rules, and one draw needn't show every extreme that they name: `tile_counts`: some tile list uses all 384 slots. `tile_rows`: positions may repeat within a list and between lists.
All inputs are finite; a program needn't handle non-finite values.
Results may differ from a plain program's by a relative error of at most 0.0029.
Values may be sent and summed in bfloat16 or wider, within the bound.
A program may use at most 128 MiB of HBM per device.

v0:
```python
import math

import jax
import jax.numpy as jnp
from jax import lax
from jax.sharding import PartitionSpec as P

step_tiles = 16


def make_adder(grad_tiles, values, row_list, col_list, lower, upper, grouped):

    def add_tiles(step_index, column_sums):
        first_slot = step_index * grouped
        tile_block = lax.dynamic_slice_in_dim(values, first_slot, grouped, 0)
        row_index = lax.dynamic_slice_in_dim(row_list, first_slot, grouped, 0)
        col_index = lax.dynamic_slice_in_dim(col_list, first_slot, grouped, 0)
        selected = jnp.take(grad_tiles, row_index, axis=0)
        products = jnp.einsum(
            "tij,tid->tjd", tile_block, selected, preferred_element_type=jnp.float32
        )
        slot_ids = first_slot + jnp.arange(grouped, dtype=jnp.int32)
        in_use = (slot_ids >= lower) & (slot_ids < upper)
        products = jnp.where(in_use[:, None, None], products, jnp.zeros_like(products))
        return column_sums.at[col_index].add(products)

    return add_tiles


def body(grad_out, tile_vals, tile_rows, tile_cols, tile_counts):
    rounded = grad_out.astype(jnp.bfloat16)
    row_block = lax.all_gather(rounded, ("col", "rep"), axis=0, tiled=True)
    tile_width = tile_vals.shape[1]
    features = row_block.shape[1]
    capacity = tile_vals.shape[0]
    half_slots = capacity // 2
    grouped = math.gcd(step_tiles, half_slots)
    grad_tiles = row_block.reshape(row_block.shape[0] // tile_width, tile_width, features)
    column_rows = grad_out.shape[0] * lax.axis_size("row") * lax.axis_size("rep")
    column_tiles = column_rows // tile_width
    used_slots = tile_counts[0]
    column_sums = jnp.zeros((column_tiles, tile_width, features), jnp.float32)
    own_adder = make_adder(grad_tiles, tile_vals, tile_rows, tile_cols, 0, used_slots, grouped)
    column_sums = lax.fori_loop(0, (used_slots + grouped - 1) // grouped, own_adder, column_sums)
    flattened = column_sums.reshape(column_rows, features)
    paired = lax.psum(flattened, "rep")
    row_share = lax.psum_scatter(paired, "row", scatter_dimension=0, tiled=True)
    own_rows = row_share.shape[0] // lax.axis_size("rep")
    return lax.dynamic_slice_in_dim(row_share, lax.axis_index("rep") * own_rows, own_rows, 0)


def solution(mesh):
    placed = (
        P(("row", "col", "rep"), None),
        P(("row", "col", "rep"), None, None),
        P(("row", "col", "rep")),
        P(("row", "col", "rep")),
        P(("row", "col", "rep")),
    )
    return jax.shard_map(
        body, mesh=mesh, in_specs=placed, out_specs=P(("col", "row", "rep"), None), check_vma=False
    )
```

profile of v0, /device:TPU:1, one launch (start us, length us, event | category | flops | bytes accessed | tf_op | source)
XLA Modules:
  0.0 520.0 jit_solution(6318619356433265061)
XLA Ops:
  6.5 0.0 all-gather.2.cloned.1.call-start
  6.5 1.6 convert_element_type.3
  8.2 0.0 all-gather.2.cloned.1.call-update
  8.2 0.0 reduce-scatter.2.cloned.1.call-start
  8.9 104.3 %all-gather.2.cloned.1.call-done = bf16[8192,256]{1,0:T(8,128)(2,1)} async-done(((bf16[256,256]{1,0:T(8,128)(2,1)}), bf16[8192,256]{1,0:T(8,128)(2,1)}) %all-gather.2.cloned.1.call-update) | async-done | bytes 4194320 | tf_op jit(solution)/shard_map/all_gather | solution.py:32
  113.2 2.5 broadcast_in_dim.27
  115.6 33.2 %while.10 = (s32[]{:T(128)}, f32[32,128,256]{2,1,0:T(8,128)}, s32[]{:T(128)}, s32[384]{0:T(512)}, s32[]{:T(128)}, /*index=5*/bf16[384,128,128]{2,1,0:T(8,128)(2,...) while((s32[]{:T(128)}, f32[32,128,256]{2,1,0:T(8,128)}, ...), condition=%wide.region_2.3_spmd, body=%wide.region_0.2_spmd.sunk | while | flops 135791824 | bytes 12063415 | solution.py:44
  115.6 1.4 compare_and_fusion.3
  117.0 2.8 gather_fusion
  119.8 1.6 convolution_select_fusion.2
  121.4 0.8 compare_select_fusion.4
  122.2 4.5 scatter_fusion
  126.7 1.4 compare_and_fusion.3
  128.1 2.8 gather_fusion
  130.9 1.6 convolution_select_fusion.2
  132.5 0.8 compare_select_fusion.4
  133.3 4.5 scatter_fusion
  137.7 1.4 compare_and_fusion.3
  139.2 2.8 gather_fusion
  142.0 1.6 convolution_select_fusion.2
  143.5 0.8 compare_select_fusion.4
  144.3 4.5 scatter_fusion
  148.8 0.0 reduce-scatter.2.cloned.1.call-update
  148.8 0.0 all-reduce.2.cloned.1.call-start
  148.9 320.0 %reduce-scatter.2.cloned.1.call-done = f32[512,256]{1,0:T(8,128)} async-done(((f32[4096,256]{1,0:T(8,128)}), f32[512,256]{1,0:T(8,128)}) %reduce-scatter.2.cloned.1.call-update) | async-done | bytes 524304 | tf_op jit(solution)/shard_map/reduce_scatter | solution.py:47
  468.9 0.0 all-reduce.2.cloned.1.call-update
  468.9 42.9 %all-reduce.2.cloned.1.call-done = f32[512,256]{1,0:T(8,128)} async-done(((f32[512,256]{1,0:T(8,128)}), f32[512,256]{1,0:T(8,128)}) %all-reduce.2.cloned.1.call-update) | async-done | bytes 524304 | tf_op jit(solution)/shard_map/psum | solution.py:46
  511.8 1.7 constant_dynamic-slice_fusion
  (3 shorter events, 0.0 us)
Async XLA Ops:
  6.5 106.6 %all-gather.2.cloned.1.call-start = ((), (), s32[]{:S(2)}) async-start(), calls=%async_computation.1 | async-start | bytes 4325376 | tf_op jit(solution)/shard_map/all_gather | solution.py:32
  8.2 460.7 %reduce-scatter.2.cloned.1.call-start = ((), (), s32[]{:S(2)}) async-start(), calls=%async_computation.2 | async-start | bytes 4718592 | tf_op jit(solution)/shard_map/reduce_scatter | solution.py:47
  148.8 363.0 %all-reduce.2.cloned.1.call-start = ((), (), s32[]{:S(2)}) async-start(), calls=%async_computation.3 | async-start | bytes 1048576 | tf_op jit(solution)/shard_map/psum | solution.py:46
Sparse Core Ops, SparseCore 0:
  9.2 103.9 all-gather.1
  149.0 319.8 reduce-scatter.1
  471.5 40.3 all-reduce.1
where the time goes:
time: 524 us; the launch traced here: 520 us
  waiting for transfers between devices  467 us (89%)
  other arithmetic  21.6 us (4%)
  between operations  13.8 us (3%)
  local copies, waits for them, and re-layouts  12.5 us (2%)
    reduce_scatter x1, waiting for transfers between devices, body(): row_share = lax.psum_scatter(paired, 'row', scatter_dimension=0, tiled=True)  320 us
    all_gather x1, waiting for transfers between devices, body(): row_block = lax.all_gather(rounded, ('col', 'rep'), axis=0, tiled=True)  104 us
    psum x1, waiting for transfers between devices, body(): paired = lax.psum(flattened, 'rep')  42.9 us
    scatter-add x3, other arithmetic, add_tiles(): return column_sums.at[col_index].add(products)  13.5 us
  transfers between devices with their start and end apart: 3, of which 3 were waited for; matrix products, arithmetic and copies ran while one was open for 0% of the time, Pallas kernels for 0%

commit v1 on v0

v1 whole, which is shorter than its diff:
```python
import functools

import jax
import jax.numpy as jnp
from jax import lax
from jax.experimental import pallas as pl
from jax.experimental.pallas import tpu as pltpu
from jax.sharding import PartitionSpec as P

MESH = pl.DeviceIdType.MESH
T = 128
D = 256
SLOTS = 384
PAIRS = 208
BATCH = 26
CHUNKS = (128, 128)
X, Y, Z = 4, 4, 8


def prepare(rows, cols, count, z, y):
    zs, cs, ys, ts = rows >> 3, (rows >> 2) & 1, (rows >> 1) & 1, rows & 1
    zrel = (zs - z + 8) & 7
    zslot = jnp.where(zrel < 4, 2 * zrel, jnp.where(zrel == 4, 7, 15 - 2 * zrel))
    yrel = (ys - y + 2) & 1
    place = jnp.where(cs == 0, yrel * 16 + zslot * 2 + ts, 32 + zslot * 4 + yrel * 2 + ts)

    lane = lax.broadcasted_iota(jnp.int32, (1, SLOTS), 1)
    colr = jnp.where(lane < count, cols, 64)

    def column(v):
        return jnp.transpose(jnp.broadcast_to(v, (T, SLOTS)))

    colc, placec = column(colr), column(place)
    slotc = lax.broadcasted_iota(jnp.int32, (SLOTS, T), 0)
    one, zero = jnp.int32(1), jnp.int32(0)
    lanes = lax.broadcasted_iota(jnp.int32, (SLOTS, T), 1)
    n_row = jnp.sum(jnp.where(colc == lanes, one, zero), axis=0, keepdims=True)
    pair_row = jnp.where(lax.broadcasted_iota(jnp.int32, (1, T), 1) < 32, (n_row + 1) >> 1, 0)
    pair_col = jnp.transpose(jnp.broadcast_to(pair_row, (T, T)))
    sub = lax.broadcasted_iota(jnp.int32, (T, T), 0)
    lan = lax.broadcasted_iota(jnp.int32, (T, T), 1)
    ends = jnp.sum(jnp.where(sub <= lan, pair_col, zero), axis=0, keepdims=True)
    starts = ends - pair_row
    last = jnp.where(pair_row > 0, ends - 1, PAIRS)
    wide = jnp.concatenate([colc] * (SLOTS // T), axis=1)
    si = lax.broadcasted_iota(jnp.int32, (SLOTS, SLOTS), 0)
    ti = lax.broadcasted_iota(jnp.int32, (SLOTS, SLOTS), 1)
    same = jnp.where((wide == colr) & (ti < si), 1.0, 0.0)
    rank = jnp.sum(same, axis=1, keepdims=True).astype(jnp.int32)
    mine = jnp.where(colc == lanes, jnp.broadcast_to(starts, (SLOTS, T)), zero)
    start = jnp.sum(mine.astype(jnp.float32), axis=1, keepdims=True).astype(jnp.int32)
    pos = jnp.where(colc[:, :1] < 32, 2 * start + rank, -1)
    opens = jnp.where(rank == 0, one, zero)
    parts = [[], [], []]
    for block in range(4):
        target = lanes + block * T
        hit = jnp.broadcast_to(pos, (SLOTS, T)) == target
        parts[0].append(SLOTS + jnp.sum(jnp.where(hit, slotc - SLOTS, zero), axis=0, keepdims=True))
        parts[1].append(jnp.sum(jnp.where(hit, placec, zero), axis=0, keepdims=True))
        parts[2].append(jnp.sum(jnp.where(hit, jnp.broadcast_to(opens, (SLOTS, T)), zero), axis=0, keepdims=True))
    out = [jnp.concatenate(p, axis=1) for p in parts]
    out.append(jnp.concatenate([last] * 4, axis=1))
    return jnp.concatenate(out + out, axis=0)


def kernel(grad_hbm, tiles_hbm, rows_hbm, cols_hbm, count_hbm, out_ref, *scratch):
    F = len(CHUNKS)
    it = iter(scratch)
    grad, rows, cols, count, tiles, table, meta, sums = (next(it) for _ in range(8))
    G = [next(it) for _ in range(F)]
    SB = [next(it) for _ in range(F)]
    R1 = [next(it) for _ in range(F)]
    SC = [next(it) for _ in range(F)]
    R2 = [next(it) for _ in range(F)]
    own = [next(it) for _ in range(F)]
    local, zsem, ysem, csem, gsend, s1, s2, rs1, rs2 = (next(it) for _ in range(9))

    row, col, rep = lax.axis_index("row"), lax.axis_index("col"), lax.axis_index("rep")
    x, y = row // 2, lax.rem(row, 2) * 2 + rep
    z, core = col // 2, lax.rem(col, 2)

    def device(x, y, z, core):
        return (x * 2 + y // 2, z * 2 + core, lax.rem(y, 2))

    up = device(x, y, lax.rem(z + 1, Z), core)
    down = device(x, y, lax.rem(z + Z - 1, Z), core)
    across = device(x, y + 1 - 2 * rep, z, core)
    sibling = device(x, y, z, 1 - core)
    along_x = [device(lax.rem(x + k, X), y, z, core) for k in range(1, X)]
    along_y = [device(x, lax.rem(y + k, Y), z, core) for k in range(1, Y)]

    barrier = pltpu.get_barrier_semaphore()
    for other in [up, down, sibling] + along_x + along_y:
        pl.semaphore_signal(barrier, inc=1, device_id=other, device_id_type=MESH)

    loads = [
        pltpu.make_async_copy(grad_hbm, grad, local.at[0]),
        pltpu.make_async_copy(rows_hbm, rows, local.at[1]),
        pltpu.make_async_copy(cols_hbm, cols, local.at[2]),
        pltpu.make_async_copy(count_hbm, count, local.at[3]),
        pltpu.make_async_copy(tiles_hbm, tiles.at[pl.ds(0, SLOTS)], local.at[4]),
    ]
    for load in loads:
        load.start()
    tiles[SLOTS] = jnp.zeros((T, T), jnp.bfloat16)
    sums[PAIRS] = jnp.zeros(sums.shape[1:], jnp.bfloat16)

    loads[0].wait()
    base = core * 32
    firsts = [sum(CHUNKS[:m]) for m in range(F)]
    for t in range(2):
        flipped = jnp.transpose(grad[t * T : (t + 1) * T, :]).astype(jnp.bfloat16)
        for m in range(F):
            G[m][base + t] = flipped[firsts[m] : firsts[m] + CHUNKS[m]]
    pl.semaphore_wait(barrier, 9)

    def tiles_to(m, start, stop, n, to, sem):
        return pltpu.make_async_remote_copy(
            src_ref=G[m].at[pl.ds(start, n)],
            dst_ref=G[m].at[pl.ds(stop, n)],
            send_sem=gsend.at[m],
            recv_sem=sem,
            device_id=to,
            device_id_type=MESH,
        )

    def z_send(m, which, k, c):
        to = up if which == 0 else down
        nxt = 7 if k in (5, 6) else (k + 2 if k else 1 + which)
        at, n = (2, 2) if c == 0 else (4, 4)
        off = 32 * c
        tiles_to(m, off + at * k, off + at * nxt, n, to, zsem.at[m, nxt]).start()

    def z_wait(m, k, c):
        n = 2 if c == 0 else 4
        at = 2 * k if c == 0 else 32 + 4 * k
        tiles_to(m, at, at, n, up, zsem.at[m, k]).wait_recv()

    def y_send(m, start, n):
        tiles_to(m, start, start + 16, n, across, ysem.at[m]).start()

    def c_send(m, start, n):
        tiles_to(m, start, start, n, sibling, csem.at[m]).start()

    def gather(m, e):
        def zero():
            if e == 0:
                z_send(m, 0, 0, 0)
                z_send(m, 1, 0, 0)
                y_send(m, 0, 2)
            elif e in (1, 2):
                z_wait(m, 2 * e - 1, 0)
                z_send(m, 0, 2 * e - 1, 0)
                z_wait(m, 2 * e, 0)
                z_send(m, 1, 2 * e, 0)
                y_send(m, 4 * e - 2, 4)
            elif e == 3:
                z_wait(m, 5, 0)
                z_send(m, 0, 5, 0)
                z_wait(m, 6, 0)
                y_send(m, 10, 4)
            elif e == 4:
                z_wait(m, 7, 0)
                y_send(m, 14, 2)
                c_send(m, 0, 16)
            elif e == 5:
                tiles_to(m, 16, 16, 16, across, ysem.at[m]).wait_recv()
                c_send(m, 16, 16)
            elif e == 6:
                tiles_to(m, 32, 32, 32, sibling, csem.at[m]).wait_recv()

        def one():
            if e == 0:
                tiles_to(m, 32, 34, 2, across, ysem.at[m]).start()
            elif e == 1:
                tiles_to(m, 34, 34, 2, across, ysem.at[m]).wait_recv()
                z_send(m, 0, 0, 1)
                z_send(m, 1, 0, 1)
            elif e in (2, 3):
                z_wait(m, 2 * e - 3, 1)
                z_send(m, 0, 2 * e - 3, 1)
                z_wait(m, 2 * e - 2, 1)
                z_send(m, 1, 2 * e - 2, 1)
            elif e == 4:
                z_wait(m, 6, 1)
                z_send(m, 1, 6, 1)
                z_wait(m, 5, 1)
                c_send(m, 32, 28)
            elif e == 5:
                z_wait(m, 7, 1)
                c_send(m, 60, 4)
            elif e == 6:
                tiles_to(m, 0, 0, 32, sibling, csem.at[m]).wait_recv()

        pl.when(core == 0)(zero)
        pl.when(core == 1)(one)

    def multiply(m, hooks):
        M = CHUNKS[m]

        def step(b, run):
            for at, todo in hooks.items():
                pl.when(b == at)(todo)
            products, opens = [], []
            for q in range(BATCH):
                s = 2 * (b * BATCH + q)
                left = jnp.concatenate([G[m][meta[1, s]], G[m][meta[1, s + 1]]], axis=1)
                right = jnp.concatenate([tiles[meta[0, s]], tiles[meta[0, s + 1]]], axis=0)
                products.append(jnp.dot(left, right, preferred_element_type=jnp.float32))
                opens.append(meta[2, s])
            for q in range(BATCH):
                run = jnp.where(opens[q] != 0, 0.0, run) + products[q]
                sums[b * BATCH + q, :M] = run.astype(jnp.bfloat16)
            return run

        lax.fori_loop(0, PAIRS // BATCH, step, jnp.zeros((M, T), jnp.float32))

    def ring(buf_from, buf_to, i, k, n, ssem, rsem, to):
        return pltpu.make_async_remote_copy(
            src_ref=buf_from.at[i],
            dst_ref=buf_to.at[n],
            send_sem=ssem,
            recv_sem=rsem,
            device_id=to,
            device_id_type=MESH,
        )

    order = (1, 0, 2)

    def reduce(m, e):
        M, H = CHUNKS[m], CHUNKS[m] // 2
        if e == 0:
            for c in range(32):
                v = sums[meta[3, c], :M]
                xd, yd, t = c // 8, c // 2 % 4, c % 2
                SB[m][xd, 2 * yd + t] = v[:H]
                SB[m][4 + yd, 2 * xd + t] = v[H:]
            for k in order:
                ring(SB[m], R1[m], lax.rem(x + k + 1, X), k, k, s1.at[m], rs1.at[m], along_x[k]).start()
                ring(SB[m], R1[m], 4 + lax.rem(y + k + 1, Y), k, 3 + k, s1.at[m], rs1.at[m], along_y[k]).start()
        elif e == 1:
            everything = pltpu.make_async_remote_copy(
                src_ref=R1[m], dst_ref=R1[m], send_sem=s1.at[m], recv_sem=rs1.at[m], device_id=up, device_id_type=MESH
            )
            everything.wait_recv()
            for side, me in ((0, x), (1, y)):
                total = SB[m][4 * side + me].astype(jnp.float32)
                for k in range(3):
                    total += R1[m][3 * side + k].astype(jnp.float32)
                for d in range(4):
                    SC[m][4 * side + d] = total[2 * d : 2 * d + 2].astype(jnp.bfloat16)
                mine = SB[m][4 * side + me, pl.ds(2 * (y if side == 0 else x), 2)].astype(jnp.float32)
                for k in range(3):
                    mine += R1[m][3 * side + k, pl.ds(2 * (y if side == 0 else x), 2)].astype(jnp.float32)
                own[m][side] = mine
            for k in order:
                ring(SC[m], R2[m], lax.rem(y + k + 1, Y), k, k, s2.at[m], rs2.at[m], along_y[k]).start()
                ring(SC[m], R2[m], 4 + lax.rem(x + k + 1, X), k, 3 + k, s2.at[m], rs2.at[m], along_x[k]).start()
        elif e == 2:
            everything = pltpu.make_async_remote_copy(
                src_ref=R2[m], dst_ref=R2[m], send_sem=s2.at[m], recv_sem=rs2.at[m], device_id=up, device_id_type=MESH
            )
            everything.wait_recv()
            for side in range(2):
                total = own[m][side]
                for k in range(3):
                    total += R2[m][3 * side + k].astype(jnp.float32)
                out_ref[:, pl.ds(firsts[m] + side * H, H), :] = total

    def sent(m):
        tiles_to(m, 0, 0, 62, up, csem.at[m]).wait_send()
        pltpu.make_async_remote_copy(
            src_ref=R1[m], dst_ref=R1[m], send_sem=s1.at[m], recv_sem=rs1.at[m], device_id=up, device_id_type=MESH
        ).wait_send()
        pltpu.make_async_remote_copy(
            src_ref=R2[m], dst_ref=R2[m], send_sem=s2.at[m], recv_sem=rs2.at[m], device_id=up, device_id_type=MESH
        ).wait_send()

    gather(0, 0)
    for load in loads[1:4]:
        load.wait()
    table[...] = prepare(rows[...], cols[...], count[0], z, rep)
    to_scalars = pltpu.make_async_copy(table, meta, local.at[5])
    to_scalars.start()
    for e in range(1, 6):
        gather(0, e)
        gather(1, e - 1)
    gather(0, 6)
    to_scalars.wait()
    loads[4].wait()
    multiply(0, {2: lambda: gather(1, 5)})
    reduce(0, 0)
    gather(1, 6)
    multiply(1, {6: lambda: reduce(0, 1)})
    reduce(1, 0)
    reduce(0, 2)
    reduce(1, 1)
    reduce(1, 2)
    for m in range(F):
        sent(m)


def body(grad_out, tile_vals, tile_rows, tile_cols, tile_counts):
    vmem, bf16 = pltpu.VMEM, jnp.bfloat16
    F = len(CHUNKS)
    anywhere = pl.BlockSpec(memory_space=pl.ANY)
    shares = pl.pallas_call(
        kernel,
        out_shape=jax.ShapeDtypeStruct((2, D, T), jnp.float32),
        in_specs=[anywhere] * 5,
        out_specs=pl.BlockSpec(memory_space=vmem),
        scratch_shapes=[
            vmem((D, D), jnp.float32),
            vmem((1, SLOTS), jnp.int32),
            vmem((1, SLOTS), jnp.int32),
            pltpu.SMEM((1,), jnp.int32),
            vmem((SLOTS + 1, T, T), bf16),
            vmem((8, 512), jnp.int32),
            pltpu.SMEM((8, 512), jnp.int32),
            vmem((PAIRS + 1, max(CHUNKS), T), bf16),
        ]
        + [vmem((64, M, T), bf16) for M in CHUNKS]
        + [vmem((8, 8, M // 2, T), bf16) for M in CHUNKS]
        + [vmem((6, 8, M // 2, T), bf16) for M in CHUNKS]
        + [vmem((8, 2, M // 2, T), bf16) for M in CHUNKS]
        + [vmem((6, 2, M // 2, T), bf16) for M in CHUNKS]
        + [vmem((2, 2, M // 2, T), jnp.float32) for M in CHUNKS]
        + [
            pltpu.SemaphoreType.DMA((6,)),
            pltpu.SemaphoreType.DMA((F, 8)),
        ]
        + [pltpu.SemaphoreType.DMA((F,)) for _ in range(7)],
        compiler_params=pltpu.CompilerParams(
            collective_id=0, has_side_effects=True, vmem_limit_bytes=56 * 2**20
        ),
    )(grad_out, tile_vals, tile_rows.reshape(1, SLOTS), tile_cols.reshape(1, SLOTS), tile_counts)
    return jnp.transpose(shares, (0, 2, 1)).reshape(2 * T, D)


def solution(mesh):
    placed = (
        P(("row", "col", "rep"), None),
        P(("row", "col", "rep"), None, None),
        P(("row", "col", "rep")),
        P(("row", "col", "rep")),
        P(("row", "col", "rep")),
    )
    return jax.shard_map(
        body, mesh=mesh, in_specs=placed, out_specs=P(("col", "row", "rep"), None), check_vma=False
    )
```

time: 524 us -> 63.6 us (0.12)
  waiting for transfers between devices: 467 us -> 0 us
  Pallas kernels: 0 us -> 58.5 us
  other arithmetic: 21.6 us -> 0 us
  between operations: 13.8 us -> 0.66 us
  local copies, waits for them, and re-layouts: 12.5 us -> 4.29 us
    reduce_scatter x1 -> x0, waiting for transfers between devices: 320 us -> none  [body(): row_share = lax.psum_scatter(paired, 'row', scatter_dimension=0, tiled=True)]
    all_gather x1 -> x0, waiting for transfers between devices: 104 us -> none  [body(): row_block = lax.all_gather(rounded, ('col', 'rep'), axis=0, tiled=True)]
    pallas_call x0 -> x1, Pallas kernels: none -> 58.5 us  [body(): pl.pallas_call(kernel, out_shape=jax.ShapeDtypeStruct((2, D, T), jnp.floa...]
    psum x1 -> x0, waiting for transfers between devices: 42.9 us -> none  [body(): paired = lax.psum(flattened, 'rep')]
    scatter-add x3 -> x0, other arithmetic: 13.5 us -> none  [add_tiles(): return column_sums.at[col_index].add(products)]
    gather x3 -> x0, local copies, waits for them, and re-layouts: 8.4 us -> none  [add_tiles(): selected = jnp.take(grad_tiles, row_index, axis=0)]
  transfers between devices with their start and end apart: 3 -> 0, of which waited for: 3 -> 0; matrix products, arithmetic and copies ran while one was open for 0% -> 0% of each run, Pallas kernels for 0% -> 0%
where the time goes in v1:
time: 63.6 us; the launch traced here: 63.4 us
  Pallas kernels  58.5 us (92%)
  local copies, waits for them, and re-layouts  4.29 us (7%)
  between operations  0.66 us (1%)
    pallas_call x1, Pallas kernels, body(): pl.pallas_call(kernel, out_shape=jax.ShapeDtypeStruct((2, D, T), jnp.floa...  58.5 us
    transpose x1, local copies, waits for them, and re-layouts, body(): return jnp.transpose(shares, (0, 2, 1)).reshape(2 * T, D)  1.79 us

profile of v1, /device:TPU:1, one launch (start us, length us, event | category | flops | bytes accessed | tf_op | source)
XLA Modules:
  0.0 63.4 jit_solution(3593417049335742012)
XLA Ops:
  0.7 1.2 %reshape.9.rows_hbm = s32[1,384]{1,0:T(1,128)} reshape(s32[384]{0:T(512)} %param.7) | data formatting | bytes 3072 | tf_op jit(solution)/shard_map/reshape | solution.py:336
  1.9 1.3 %reshape.10.cols_hbm = s32[1,384]{1,0:T(1,128)} reshape(s32[384]{0:T(512)} %param.8) | data formatting | bytes 3072 | tf_op jit(solution)/shard_map/reshape | solution.py:336
  3.2 58.5 %shard_map.55 = f32[2,256,128]{2,1,0:T(8,128)} custom-call(f32[256,256]{1,0:T(8,128)} %grad_hbm.1, bf16[384,128,128]{2,1,0:T(8,128)(2,1)} %tiles_hbm.1, s32[1,384]{1,0:T(1,128)} %reshape.9.rows_hbm, s32[1,384]{1,0:T(1,128)} %reshape.10.cols_hbm, s32[1]{0:T(128)S(6)} %copy.7.count_hbm), custom_call_target="tpu_custom_call" | custom-call | tf_op jit(solution)/shard_map/pallas_call | solution.py:307
  61.6 1.8 %copy.6 = f32[2,128,256]{2,1,0:T(8,128)} copy(f32[2,128,256]{1,2,0:T(8,128)} %bitcast.2) | data formatting | bytes 524288 | tf_op jit(solution)/shard_map/transpose | solution.py:337

commit v2 on v1

--- a/solution.py
+++ b/solution.py
@@ -12,8 +12,9 @@
 D = 256
 SLOTS = 384
 PAIRS = 208
-BATCH = 26
-CHUNKS = (128, 128)
+BATCH = 52
+CHUNKS = (64, 64, 64, 64)
+PLAN = [('g', 0, 0), ('g', 1, 0), ('g', 2, 0), ('g', 3, 0), ('p', 0, 0), ('g', 0, 1), ('g', 1, 1), ('g', 2, 1), ('g', 3, 1), ('g', 0, 2), ('g', 1, 2), ('g', 2, 2), ('g', 3, 2), ('g', 0, 3), ('g', 1, 3), ('g', 2, 3), ('g', 3, 3), ('g', 0, 4), ('g', 1, 4), ('g', 2, 4), ('g', 3, 4), ('g', 0, 5), ('g', 1, 5), ('g', 2, 5), ('g', 3, 5), ('g', 0, 6), ('w', 0, 0), ('m', 0, []), ('r', 0, 0), ('g', 1, 6), ('m', 1, []), ('r', 1, 0), ('g', 2, 6), ('m', 2, [(2, ('r', 0, 1))]), ('r', 2, 0), ('g', 3, 6), ('m', 3, [(2, ('r', 1, 1)), (3, ('r', 0, 2))]), ('r', 3, 0), ('r', 2, 1), ('r', 1, 2), ('r', 3, 1), ('r', 2, 2), ('r', 3, 2)]
 X, Y, Z = 4, 4, 8
 
 
@@ -86,11 +87,12 @@
     down = device(x, y, lax.rem(z + Z - 1, Z), core)
     across = device(x, y + 1 - 2 * rep, z, core)
     sibling = device(x, y, z, 1 - core)
+    diagonal = device(x, y + 1 - 2 * rep, z, 1 - core)
     along_x = [device(lax.rem(x + k, X), y, z, core) for k in range(1, X)]
     along_y = [device(x, lax.rem(y + k, Y), z, core) for k in range(1, Y)]
 
     barrier = pltpu.get_barrier_semaphore()
-    for other in [up, down, sibling] + along_x + along_y:
+    for other in [up, down, sibling, diagonal] + along_x + along_y:
         pl.semaphore_signal(barrier, inc=1, device_id=other, device_id_type=MESH)
 
     loads = [
@@ -112,7 +114,7 @@
         flipped = jnp.transpose(grad[t * T : (t + 1) * T, :]).astype(jnp.bfloat16)
         for m in range(F):
             G[m][base + t] = flipped[firsts[m] : firsts[m] + CHUNKS[m]]
-    pl.semaphore_wait(barrier, 9)
+    pl.semaphore_wait(barrier, 10)
 
     def tiles_to(m, start, stop, n, to, sem):
         return pltpu.make_async_remote_copy(
@@ -136,8 +138,8 @@
         at = 2 * k if c == 0 else 32 + 4 * k
         tiles_to(m, at, at, n, up, zsem.at[m, k]).wait_recv()
 
-    def y_send(m, start, n):
-        tiles_to(m, start, start + 16, n, across, ysem.at[m]).start()
+    def y_send(m, start, n, part=0):
+        tiles_to(m, start, start + 16, n, across, ysem.at[m, part]).start()
 
     def c_send(m, start, n):
         tiles_to(m, start, start, n, sibling, csem.at[m]).start()
@@ -161,21 +163,25 @@
                 y_send(m, 10, 4)
             elif e == 4:
                 z_wait(m, 7, 0)
-                y_send(m, 14, 2)
+                y_send(m, 14, 2, 1)
+                tiles_to(m, 14, 30, 2, diagonal, csem.at[m]).start()
                 c_send(m, 0, 16)
             elif e == 5:
-                tiles_to(m, 16, 16, 16, across, ysem.at[m]).wait_recv()
-                c_send(m, 16, 16)
+                tiles_to(m, 16, 16, 14, across, ysem.at[m, 0]).wait_recv()
+                c_send(m, 16, 14)
             elif e == 6:
+                tiles_to(m, 30, 30, 2, across, ysem.at[m, 1]).wait_recv()
                 tiles_to(m, 32, 32, 32, sibling, csem.at[m]).wait_recv()
 
         def one():
             if e == 0:
-                tiles_to(m, 32, 34, 2, across, ysem.at[m]).start()
+                tiles_to(m, 32, 34, 2, across, ysem.at[m, 0]).start()
+                tiles_to(m, 32, 36, 2, up, zsem.at[m, 1]).start()
+                tiles_to(m, 32, 40, 2, down, zsem.at[m, 2]).start()
             elif e == 1:
-                tiles_to(m, 34, 34, 2, across, ysem.at[m]).wait_recv()
-                z_send(m, 0, 0, 1)
-                z_send(m, 1, 0, 1)
+                tiles_to(m, 34, 34, 2, across, ysem.at[m, 0]).wait_recv()
+                tiles_to(m, 34, 38, 2, up, zsem.at[m, 1]).start()
+                tiles_to(m, 34, 42, 2, down, zsem.at[m, 2]).start()
             elif e in (2, 3):
                 z_wait(m, 2 * e - 3, 1)
                 z_send(m, 0, 2 * e - 3, 1)
@@ -200,7 +206,12 @@
 
         def step(b, run):
             for at, todo in hooks.items():
-                pl.when(b == at)(todo)
+
+                @pl.when(b == at)
+                def _():
+                    for item in todo:
+                        do(item)
+
             products, opens = [], []
             for q in range(BATCH):
                 s = 2 * (b * BATCH + q)
@@ -215,17 +226,17 @@
 
         lax.fori_loop(0, PAIRS // BATCH, step, jnp.zeros((M, T), jnp.float32))
 
-    def ring(buf_from, buf_to, i, k, n, ssem, rsem, to):
+    def whole(ref, ssem, rsem):
         return pltpu.make_async_remote_copy(
-            src_ref=buf_from.at[i],
-            dst_ref=buf_to.at[n],
-            send_sem=ssem,
-            recv_sem=rsem,
-            device_id=to,
-            device_id_type=MESH,
+            src_ref=ref, dst_ref=ref, send_sem=ssem, recv_sem=rsem, device_id=up, device_id_type=MESH
         )
 
-    order = (1, 0, 2)
+    def hop(src, dst, ssem, rsem, to):
+        return pltpu.make_async_remote_copy(
+            src_ref=src, dst_ref=dst, send_sem=ssem, recv_sem=rsem, device_id=to, device_id_type=MESH
+        )
+
+    sides = ((0, x, along_x, y, along_y), (1, y, along_y, x, along_x))
 
     def reduce(m, e):
         M, H = CHUNKS[m], CHUNKS[m] // 2
@@ -235,32 +246,29 @@
                 xd, yd, t = c // 8, c // 2 % 4, c % 2
                 SB[m][xd, 2 * yd + t] = v[:H]
                 SB[m][4 + yd, 2 * xd + t] = v[H:]
-            for k in order:
-                ring(SB[m], R1[m], lax.rem(x + k + 1, X), k, k, s1.at[m], rs1.at[m], along_x[k]).start()
-                ring(SB[m], R1[m], 4 + lax.rem(y + k + 1, Y), k, 3 + k, s1.at[m], rs1.at[m], along_y[k]).start()
+            for k in (1, 0, 2):
+                for side, me, along, _, _ in sides:
+                    block = 4 * side + lax.rem(me + k + 1, 4)
+                    hop(SB[m].at[block], R1[m].at[3 * side + k], s1.at[m], rs1.at[m], along[k]).start()
         elif e == 1:
-            everything = pltpu.make_async_remote_copy(
-                src_ref=R1[m], dst_ref=R1[m], send_sem=s1.at[m], recv_sem=rs1.at[m], device_id=up, device_id_type=MESH
-            )
-            everything.wait_recv()
-            for side, me in ((0, x), (1, y)):
+            whole(R1[m], s1.at[m], rs1.at[m]).wait_recv()
+            for side, me, _, place, _ in sides:
                 total = SB[m][4 * side + me].astype(jnp.float32)
                 for k in range(3):
                     total += R1[m][3 * side + k].astype(jnp.float32)
                 for d in range(4):
                     SC[m][4 * side + d] = total[2 * d : 2 * d + 2].astype(jnp.bfloat16)
-                mine = SB[m][4 * side + me, pl.ds(2 * (y if side == 0 else x), 2)].astype(jnp.float32)
+                at = pl.ds(2 * place, 2)
+                mine = SB[m][4 * side + me, at].astype(jnp.float32)
                 for k in range(3):
-                    mine += R1[m][3 * side + k, pl.ds(2 * (y if side == 0 else x), 2)].astype(jnp.float32)
+                    mine += R1[m][3 * side + k, at].astype(jnp.float32)
                 own[m][side] = mine
-            for k in order:
-                ring(SC[m], R2[m], lax.rem(y + k + 1, Y), k, k, s2.at[m], rs2.at[m], along_y[k]).start()
-                ring(SC[m], R2[m], 4 + lax.rem(x + k + 1, X), k, 3 + k, s2.at[m], rs2.at[m], along_x[k]).start()
+            for k in (1, 0, 2):
+                for side, _, _, place, along in sides:
+                    block = 4 * side + lax.rem(place + k + 1, 4)
+                    hop(SC[m].at[block], R2[m].at[3 * side + k], s2.at[m], rs2.at[m], along[k]).start()
         elif e == 2:
-            everything = pltpu.make_async_remote_copy(
-                src_ref=R2[m], dst_ref=R2[m], send_sem=s2.at[m], recv_sem=rs2.at[m], device_id=up, device_id_type=MESH
-            )
-            everything.wait_recv()
+            whole(R2[m], s2.at[m], rs2.at[m]).wait_recv()
             for side in range(2):
                 total = own[m][side]
                 for k in range(3):
@@ -269,33 +277,32 @@
 
     def sent(m):
         tiles_to(m, 0, 0, 62, up, csem.at[m]).wait_send()
-        pltpu.make_async_remote_copy(
-            src_ref=R1[m], dst_ref=R1[m], send_sem=s1.at[m], recv_sem=rs1.at[m], device_id=up, device_id_type=MESH
-        ).wait_send()
-        pltpu.make_async_remote_copy(
-            src_ref=R2[m], dst_ref=R2[m], send_sem=s2.at[m], recv_sem=rs2.at[m], device_id=up, device_id_type=MESH
-        ).wait_send()
-
-    gather(0, 0)
-    for load in loads[1:4]:
-        load.wait()
-    table[...] = prepare(rows[...], cols[...], count[0], z, rep)
+        whole(R1[m], s1.at[m], rs1.at[m]).wait_send()
+        whole(R2[m], s2.at[m], rs2.at[m]).wait_send()
+
+    def do(item):
+        kind, m, e = item
+        if kind == "g":
+            gather(m, e)
+        elif kind == "r":
+            reduce(m, e)
+        elif kind == "p":
+            for load in loads[1:4]:
+                load.wait()
+            table[...] = prepare(rows[...].reshape(1, SLOTS), cols[...].reshape(1, SLOTS), count[0], z, rep)
+            to_scalars.start()
+        elif kind == "w":
+            to_scalars.wait()
+            loads[4].wait()
+        else:
+            hooks = {}
+            for at, what in e:
+                hooks.setdefault(at, []).append(what)
+            multiply(m, hooks)
+
     to_scalars = pltpu.make_async_copy(table, meta, local.at[5])
-    to_scalars.start()
-    for e in range(1, 6):
-        gather(0, e)
-        gather(1, e - 1)
-    gather(0, 6)
-    to_scalars.wait()
-    loads[4].wait()
-    multiply(0, {2: lambda: gather(1, 5)})
-    reduce(0, 0)
-    gather(1, 6)
-    multiply(1, {6: lambda: reduce(0, 1)})
-    reduce(1, 0)
-    reduce(0, 2)
-    reduce(1, 1)
-    reduce(1, 2)
+    for item in PLAN:
+        do(item)
     for m in range(F):
         sent(m)
 
@@ -311,8 +318,8 @@
         out_specs=pl.BlockSpec(memory_space=vmem),
         scratch_shapes=[
             vmem((D, D), jnp.float32),
-            vmem((1, SLOTS), jnp.int32),
-            vmem((1, SLOTS), jnp.int32),
+            vmem((SLOTS,), jnp.int32),
+            vmem((SLOTS,), jnp.int32),
             pltpu.SMEM((1,), jnp.int32),
             vmem((SLOTS + 1, T, T), bf16),
             vmem((8, 512), jnp.int32),
@@ -328,12 +335,13 @@
         + [
             pltpu.SemaphoreType.DMA((6,)),
             pltpu.SemaphoreType.DMA((F, 8)),
+            pltpu.SemaphoreType.DMA((F, 2)),
         ]
-        + [pltpu.SemaphoreType.DMA((F,)) for _ in range(7)],
+        + [pltpu.SemaphoreType.DMA((F,)) for _ in range(6)],
         compiler_params=pltpu.CompilerParams(
             collective_id=0, has_side_effects=True, vmem_limit_bytes=56 * 2**20
         ),
-    )(grad_out, tile_vals, tile_rows.reshape(1, SLOTS), tile_cols.reshape(1, SLOTS), tile_counts)
+    )(grad_out, tile_vals, tile_rows, tile_cols, tile_counts)
     return jnp.transpose(shares, (0, 2, 1)).reshape(2 * T, D)
 
 

time: 63.6 us -> 53.4 us (0.84)
  Pallas kernels: 58.5 us -> 50.8 us
  local copies, waits for them, and re-layouts: 4.29 us -> 1.79 us
    pallas_call x1, Pallas kernels: 58.5 us -> 50.8 us  [body(): pl.pallas_call(kernel, out_shape=jax.ShapeDtypeStruct((2, D, T), jnp.floa...]
    reshape x2 -> x0, local copies, waits for them, and re-layouts: 2.5 us -> none  [the longest x1 1.25 us: body(): tile_cols.reshape(1, SLOTS)]
where the time goes in v2:
time: 53.4 us; the launch traced here: 53.3 us
  Pallas kernels  50.8 us (95%)
  local copies, waits for them, and re-layouts  1.79 us (3%)
  between operations  0.66 us (1%)
    pallas_call x1, Pallas kernels, body(): pl.pallas_call(kernel, out_shape=jax.ShapeDtypeStruct((2, D, T), jnp.floa...  50.8 us
    transpose x1, local copies, waits for them, and re-layouts, body(): return jnp.transpose(shares, (0, 2, 1)).reshape(2 * T, D)  1.79 us

profile of v2, /device:TPU:1, one launch (start us, length us, event | category | flops | bytes accessed | tf_op | source)
XLA Modules:
  0.0 53.3 jit_solution(10000602889226046253)
XLA Ops:
  0.7 50.8 %shard_map.55 = f32[2,256,128]{2,1,0:T(8,128)} custom-call(f32[256,256]{1,0:T(8,128)} %grad_hbm.1, bf16[384,128,128]{2,1,0:T(8,128)(2,1)} %tiles_hbm.1, s32[384]{0:T(512)} %rows_hbm.1, s32[384]{0:T(512)} %cols_hbm.1, s32[1]{0:T(128)S(6)} %copy.7.count_hbm), custom_call_target="tpu_custom_call" | custom-call | tf_op jit(solution)/shard_map/pallas_call | solution.py:314
  51.5 1.8 %copy.6 = f32[2,128,256]{2,1,0:T(8,128)} copy(f32[2,128,256]{1,2,0:T(8,128)} %bitcast.2) | data formatting | bytes 524288 | tf_op jit(solution)/shard_map/transpose | solution.py:345

commit v3 on v2

--- a/solution.py
+++ b/solution.py
@@ -12,9 +12,19 @@
 D = 256
 SLOTS = 384
 PAIRS = 208
-BATCH = 52
-CHUNKS = (64, 64, 64, 64)
-PLAN = [('g', 0, 0), ('g', 1, 0), ('g', 2, 0), ('g', 3, 0), ('p', 0, 0), ('g', 0, 1), ('g', 1, 1), ('g', 2, 1), ('g', 3, 1), ('g', 0, 2), ('g', 1, 2), ('g', 2, 2), ('g', 3, 2), ('g', 0, 3), ('g', 1, 3), ('g', 2, 3), ('g', 3, 3), ('g', 0, 4), ('g', 1, 4), ('g', 2, 4), ('g', 3, 4), ('g', 0, 5), ('g', 1, 5), ('g', 2, 5), ('g', 3, 5), ('g', 0, 6), ('w', 0, 0), ('m', 0, []), ('r', 0, 0), ('g', 1, 6), ('m', 1, []), ('r', 1, 0), ('g', 2, 6), ('m', 2, [(2, ('r', 0, 1))]), ('r', 2, 0), ('g', 3, 6), ('m', 3, [(2, ('r', 1, 1)), (3, ('r', 0, 2))]), ('r', 3, 0), ('r', 2, 1), ('r', 1, 2), ('r', 3, 1), ('r', 2, 2), ('r', 3, 2)]
+BATCH = 104
+CHUNKS = (64, 96, 96)
+PLAN = (
+    [("g", 0, 0), ("o", 1, 0), ("g", 1, 0), ("g", 2, 0)]
+    + [("g", 0, 1), ("g", 1, 1), ("g", 2, 1), ("t", 0, 0)]
+    + [("g", 0, 2), ("g", 1, 2), ("g", 2, 2), ("p", 0, 0)]
+    + [("g", 0, 3), ("g", 1, 3), ("g", 2, 3)]
+    + [("g", 0, 4), ("g", 1, 4), ("g", 0, 5), ("g", 2, 4), ("w", 0, 0), ("g", 0, 6)]
+    + [("m", 0, [(0, ("g", 1, 5)), (1, ("g", 2, 5))]), ("r", 0, 0), ("g", 1, 6)]
+    + [("m", 1, []), ("r", 1, 0), ("g", 2, 6)]
+    + [("m", 2, [(1, ("r", 0, 1))]), ("r", 2, 0)]
+    + [("r", 0, 2), ("r", 1, 1), ("r", 2, 1), ("r", 1, 2), ("r", 2, 2)]
+)
 X, Y, Z = 4, 4, 8
 
 
@@ -96,24 +106,31 @@
         pl.semaphore_signal(barrier, inc=1, device_id=other, device_id_type=MESH)
 
     loads = [
-        pltpu.make_async_copy(grad_hbm, grad, local.at[0]),
+        pltpu.make_async_copy(grad_hbm.at[:, pl.ds(0, T)], grad.at[:, pl.ds(0, T)], local.at[0]),
         pltpu.make_async_copy(rows_hbm, rows, local.at[1]),
         pltpu.make_async_copy(cols_hbm, cols, local.at[2]),
         pltpu.make_async_copy(count_hbm, count, local.at[3]),
         pltpu.make_async_copy(tiles_hbm, tiles.at[pl.ds(0, SLOTS)], local.at[4]),
+        pltpu.make_async_copy(grad_hbm.at[:, pl.ds(T, T)], grad.at[:, pl.ds(T, T)], local.at[6]),
     ]
-    for load in loads:
-        load.start()
+    for i in (0, 5, 1, 2, 3):
+        loads[i].start()
     tiles[SLOTS] = jnp.zeros((T, T), jnp.bfloat16)
     sums[PAIRS] = jnp.zeros(sums.shape[1:], jnp.bfloat16)
 
-    loads[0].wait()
     base = core * 32
     firsts = [sum(CHUNKS[:m]) for m in range(F)]
-    for t in range(2):
-        flipped = jnp.transpose(grad[t * T : (t + 1) * T, :]).astype(jnp.bfloat16)
-        for m in range(F):
-            G[m][base + t] = flipped[firsts[m] : firsts[m] + CHUNKS[m]]
+
+    def own_part(half):
+        loads[5 * half].wait()
+        for t in range(2):
+            flipped = jnp.transpose(grad[t * T : (t + 1) * T, half * T : (half + 1) * T]).astype(jnp.bfloat16)
+            for m in range(F):
+                start, stop = max(firsts[m], half * T), min(firsts[m] + CHUNKS[m], half * T + T)
+                if start < stop:
+                    G[m][base + t, start - firsts[m] : stop - firsts[m]] = flipped[start - half * T : stop - half * T]
+
+    own_part(0)
     pl.semaphore_wait(barrier, 10)
 
     def tiles_to(m, start, stop, n, to, sem):
@@ -252,21 +269,21 @@
                     hop(SB[m].at[block], R1[m].at[3 * side + k], s1.at[m], rs1.at[m], along[k]).start()
         elif e == 1:
             whole(R1[m], s1.at[m], rs1.at[m]).wait_recv()
-            for side, me, _, place, _ in sides:
+            for side, me, _, place, after in sides:
                 total = SB[m][4 * side + me].astype(jnp.float32)
                 for k in range(3):
                     total += R1[m][3 * side + k].astype(jnp.float32)
                 for d in range(4):
                     SC[m][4 * side + d] = total[2 * d : 2 * d + 2].astype(jnp.bfloat16)
+                for k in (1, 0, 2):
+                    block = 4 * side + lax.rem(place + k + 1, 4)
+                    hop(SC[m].at[block], R2[m].at[3 * side + k], s2.at[m], rs2.at[m], after[k]).start()
+            for side, me, _, place, _ in sides:
                 at = pl.ds(2 * place, 2)
                 mine = SB[m][4 * side + me, at].astype(jnp.float32)
                 for k in range(3):
                     mine += R1[m][3 * side + k, at].astype(jnp.float32)
                 own[m][side] = mine
-            for k in (1, 0, 2):
-                for side, _, _, place, along in sides:
-                    block = 4 * side + lax.rem(place + k + 1, 4)
-                    hop(SC[m].at[block], R2[m].at[3 * side + k], s2.at[m], rs2.at[m], along[k]).start()
         elif e == 2:
             whole(R2[m], s2.at[m], rs2.at[m]).wait_recv()
             for side in range(2):
@@ -291,6 +308,10 @@
                 load.wait()
             table[...] = prepare(rows[...].reshape(1, SLOTS), cols[...].reshape(1, SLOTS), count[0], z, rep)
             to_scalars.start()
+        elif kind == "t":
+            loads[4].start()
+        elif kind == "o":
+            own_part(m)
         elif kind == "w":
             to_scalars.wait()
             loads[4].wait()
@@ -333,7 +354,7 @@
         + [vmem((6, 2, M // 2, T), bf16) for M in CHUNKS]
         + [vmem((2, 2, M // 2, T), jnp.float32) for M in CHUNKS]
         + [
-            pltpu.SemaphoreType.DMA((6,)),
+            pltpu.SemaphoreType.DMA((7,)),
             pltpu.SemaphoreType.DMA((F, 8)),
             pltpu.SemaphoreType.DMA((F, 2)),
         ]

time: 53.4 us -> 51.6 us (0.966)
  Pallas kernels: 50.8 us -> 49.1 us
    pallas_call x1, Pallas kernels: 50.8 us -> 49.1 us  [body(): pl.pallas_call(kernel, out_shape=jax.ShapeDtypeStruct((2, D, T), jnp.floa...]
where the time goes in v3:
time: 51.6 us; the launch traced here: 51.5 us
  Pallas kernels  49.1 us (95%)
  local copies, waits for them, and re-layouts  1.79 us (3%)
  between operations  0.66 us (1%)
    pallas_call x1, Pallas kernels, body(): pl.pallas_call(kernel, out_shape=jax.ShapeDtypeStruct((2, D, T), jnp.floa...  49.1 us
    transpose x1, local copies, waits for them, and re-layouts, body(): return jnp.transpose(shares, (0, 2, 1)).reshape(2 * T, D)  1.79 us

profile of v3, /device:TPU:1, one launch (start us, length us, event | category | flops | bytes accessed | tf_op | source)
XLA Modules:
  0.0 51.5 jit_solution(3656240075652559502)
XLA Ops:
  0.7 49.1 %shard_map.55 = f32[2,256,128]{2,1,0:T(8,128)} custom-call(f32[256,256]{1,0:T(8,128)} %grad_hbm.1, bf16[384,128,128]{2,1,0:T(8,128)(2,1)} %tiles_hbm.1, s32[384]{0:T(512)} %rows_hbm.1, s32[384]{0:T(512)} %cols_hbm.1, s32[1]{0:T(128)S(6)} %copy.7.count_hbm), custom_call_target="tpu_custom_call" | custom-call | tf_op jit(solution)/shard_map/pallas_call | solution.py:335
  49.7 1.8 %copy.6 = f32[2,128,256]{2,1,0:T(8,128)} copy(f32[2,128,256]{1,2,0:T(8,128)} %bitcast.2) | data formatting | bytes 524288 | tf_op jit(solution)/shard_map/transpose | solution.py:366

commit v4 on v3

--- a/solution.py
+++ b/solution.py
@@ -258,18 +258,17 @@
     def reduce(m, e):
         M, H = CHUNKS[m], CHUNKS[m] // 2
         if e == 0:
-            for c in range(32):
-                v = sums[meta[3, c], :M]
-                xd, yd, t = c // 8, c // 2 % 4, c % 2
-                SB[m][xd, 2 * yd + t] = v[:H]
-                SB[m][4 + yd, 2 * xd + t] = v[H:]
-            for k in (1, 0, 2):
-                for side, me, along, _, _ in sides:
+            for side, me, along, _, _ in sides:
+                for c in range(32):
+                    xd, yd, t = c // 8, c // 2 % 4, c % 2
+                    block, at = (xd, 2 * yd + t) if side == 0 else (4 + yd, 2 * xd + t)
+                    SB[m][block, at] = sums[meta[3, c], side * H : (side + 1) * H]
+                for k in (1, 0, 2):
                     block = 4 * side + lax.rem(me + k + 1, 4)
-                    hop(SB[m].at[block], R1[m].at[3 * side + k], s1.at[m], rs1.at[m], along[k]).start()
+                    hop(SB[m].at[block], R1[m].at[3 * side + k], s1.at[m], rs1.at[m, side], along[k]).start()
         elif e == 1:
-            whole(R1[m], s1.at[m], rs1.at[m]).wait_recv()
             for side, me, _, place, after in sides:
+                whole(R1[m].at[pl.ds(3 * side, 3)], s1.at[m], rs1.at[m, side]).wait_recv()
                 total = SB[m][4 * side + me].astype(jnp.float32)
                 for k in range(3):
                     total += R1[m][3 * side + k].astype(jnp.float32)
@@ -277,7 +276,7 @@
                     SC[m][4 * side + d] = total[2 * d : 2 * d + 2].astype(jnp.bfloat16)
                 for k in (1, 0, 2):
                     block = 4 * side + lax.rem(place + k + 1, 4)
-                    hop(SC[m].at[block], R2[m].at[3 * side + k], s2.at[m], rs2.at[m], after[k]).start()
+                    hop(SC[m].at[block], R2[m].at[3 * side + k], s2.at[m], rs2.at[m, side], after[k]).start()
             for side, me, _, place, _ in sides:
                 at = pl.ds(2 * place, 2)
                 mine = SB[m][4 * side + me, at].astype(jnp.float32)
@@ -285,8 +284,8 @@
                     mine += R1[m][3 * side + k, at].astype(jnp.float32)
                 own[m][side] = mine
         elif e == 2:
-            whole(R2[m], s2.at[m], rs2.at[m]).wait_recv()
             for side in range(2):
+                whole(R2[m].at[pl.ds(3 * side, 3)], s2.at[m], rs2.at[m, side]).wait_recv()
                 total = own[m][side]
                 for k in range(3):
                     total += R2[m][3 * side + k].astype(jnp.float32)
@@ -294,8 +293,8 @@
 
     def sent(m):
         tiles_to(m, 0, 0, 62, up, csem.at[m]).wait_send()
-        whole(R1[m], s1.at[m], rs1.at[m]).wait_send()
-        whole(R2[m], s2.at[m], rs2.at[m]).wait_send()
+        whole(R1[m], s1.at[m], rs1.at[m, 0]).wait_send()
+        whole(R2[m], s2.at[m], rs2.at[m, 0]).wait_send()
 
     def do(item):
         kind, m, e = item
@@ -358,7 +357,8 @@
             pltpu.SemaphoreType.DMA((F, 8)),
             pltpu.SemaphoreType.DMA((F, 2)),
         ]
-        + [pltpu.SemaphoreType.DMA((F,)) for _ in range(6)],
+        + [pltpu.SemaphoreType.DMA((F,)) for _ in range(4)]
+        + [pltpu.SemaphoreType.DMA((F, 2)) for _ in range(2)],
         compiler_params=pltpu.CompilerParams(
             collective_id=0, has_side_effects=True, vmem_limit_bytes=56 * 2**20
         ),

time: 51.6 us -> 51.6 us (level)
  no operation moved by 1% of the time
where the time goes in v4:
time: 51.6 us; the launch traced here: 51.5 us
  Pallas kernels  49 us (95%)
  local copies, waits for them, and re-layouts  1.79 us (3%)
  between operations  0.66 us (1%)
    pallas_call x1, Pallas kernels, body(): pl.pallas_call(kernel, out_shape=jax.ShapeDtypeStruct((2, D, T), jnp.floa...  49 us
    transpose x1, local copies, waits for them, and re-layouts, body(): return jnp.transpose(shares, (0, 2, 1)).reshape(2 * T, D)  1.79 us

profile of v4, /device:TPU:1, one launch (start us, length us, event | category | flops | bytes accessed | tf_op | source)
XLA Modules:
  0.0 51.5 jit_solution(8908865082520407186)
XLA Ops:
  0.7 49.0 %shard_map.55 = f32[2,256,128]{2,1,0:T(8,128)} custom-call(f32[256,256]{1,0:T(8,128)} %grad_hbm.1, bf16[384,128,128]{2,1,0:T(8,128)(2,1)} %tiles_hbm.1, s32[384]{0:T(512)} %rows_hbm.1, s32[384]{0:T(512)} %cols_hbm.1, s32[1]{0:T(128)S(6)} %copy.7.count_hbm), custom_call_target="tpu_custom_call" | custom-call | tf_op jit(solution)/shard_map/pallas_call | solution.py:334
  49.7 1.8 %copy.6 = f32[2,128,256]{2,1,0:T(8,128)} copy(f32[2,128,256]{1,2,0:T(8,128)} %bitcast.2) | data formatting | bytes 524288 | tf_op jit(solution)/shard_map/transpose | solution.py:366
